TPU v7x, 128 devices: a whole 4x4x4 slice. The times are simulated.
128 devices in a mesh: seq: 16 (over y, z_hi, core), head: 8 (over z_lo, x).
Axes of the slice: x: 4, y: 4, z: 4 (z_hi: 2, z_lo: 2; z = z_hi * 2 + z_lo), core: 2. Of those that a mesh axis runs over, the one named last changes fastest.
Arguments:
- queries: bfloat16 [8192, 8192], P(('seq', 'head')), may hold values from -6 to 6
- new_keys: bfloat16 [8192, 1024], P(('seq', 'head')), may hold values from -6 to 6
- new_values: bfloat16 [8192, 1024], P(('seq', 'head')), may hold values from -6 to 6
- cache_keys: bfloat16 [4096, 1024], P('seq', 'head'), may hold values from -6 to 6
- cache_values: bfloat16 [4096, 1024], P('seq', 'head'), may hold values from -6 to 6
- retrieval: int32 [8], replicated, may hold values from 0 to 1, as said below
- sinks: int32 [8], replicated, may hold values from 32 to 64, as said below
- windows: int32 [8], replicated, may hold values from 768 to 1536, as said below
Outputs:
- attended: bfloat16 [8192, 8192], P(('seq', 'head'))
Inputs may be any that keep to these rules, and one draw needn't show every extreme that they name: `retrieval`: exactly 2 of the 8 entries are 1, the others 0. `sinks`: the largest entry is exactly 64. `windows`: the largest entry is exactly 1536.
All inputs are finite; a program needn't handle non-finite values.
Results may differ from a plain program's by a relative error of at most 0.01.
Values may be sent and summed in bfloat16 or wider, within the bound.
No kernel may reach another device: no remote copies, remote signals or barrier semaphores. Data moves between devices by JAX's collectives and lax.ppermute only.
A program may use at most 448 MiB of HBM per device.

v0:
```python
import math

import jax
import jax.numpy as jnp
from jax import lax
from jax.sharding import PartitionSpec as P

HQ = 64
KVH = 8
DH = 128


def visible_mask(key_pos, query_pos, flag, sink, window):
    before = key_pos[None, :] <= query_pos[:, None]
    near = key_pos[None, :] > query_pos[:, None] - window
    return before & ((flag == 1) | (key_pos[None, :] < sink) | near)


def attend_piece(state, query_group, key_rows, value_rows, visible):
    highest, total, summed = state
    scores = jnp.einsum("tqd,rd->tqr", query_group, key_rows, preferred_element_type=jnp.float32)
    scores = scores * (1.0 / math.sqrt(DH))
    scores = jnp.where(visible[:, None, :], scores, -jnp.inf)
    fresh = jnp.maximum(highest, jnp.max(scores, -1))
    expo = jnp.exp(scores - fresh[..., None])
    total = jnp.sum(expo, -1)
    weights = expo.astype(jnp.bfloat16)
    summed = jnp.einsum("tqr,rd->tqd", weights, value_rows, preferred_element_type=jnp.float32)
    return (fresh, total, summed)


def maybe_attend(state, query_group, key_rows, value_rows, visible):
    return lax.cond(
        jnp.any(visible),
        lambda s: attend_piece(s, query_group, key_rows, value_rows, visible),
        lambda s: s,
        state,
    )


def empty_state(rows, group):
    return (
        jnp.full((rows, group), -1e30, jnp.float32),
        jnp.zeros((rows, group), jnp.float32),
        jnp.zeros((rows, group, DH), jnp.float32),
    )


def body(queries, new_keys, new_values, cache_keys, cache_values, retrieval, sinks, windows):
    heads = lax.axis_size("head")
    n_seq = lax.axis_size("seq")
    seq_index = lax.axis_index("seq")
    head_index = lax.axis_index("head")
    tok_dev = queries.shape[0]
    pre_dev = cache_keys.shape[0]
    prefix = pre_dev * n_seq
    group = HQ // KVH
    rows = tok_dev * heads
    query_pos = prefix + seq_index * rows + jnp.arange(rows, dtype=jnp.int32)
    query_x, keys_x, values_x = (
        lax.all_to_all(queries, "head", split_axis=1, concat_axis=0, tiled=True),
        lax.all_to_all(new_keys, "head", split_axis=1, concat_axis=0, tiled=True),
        lax.all_to_all(new_values, "head", split_axis=1, concat_axis=0, tiled=True),
    )
    local_kv = keys_x.shape[1] // DH
    key_block = jnp.concatenate([cache_keys, keys_x], 0)
    value_block = jnp.concatenate([cache_values, values_x], 0)
    span = pre_dev + rows
    query_groups = query_x.reshape(rows, local_kv, group, DH)
    first_head = head_index * local_kv
    start_state = tuple((empty_state(rows, group) for inner in range(local_kv)))
    key_piece = lax.all_gather(key_block, "seq", axis=0, tiled=True)
    value_piece = lax.all_gather(value_block, "seq", axis=0, tiled=True)
    count = key_piece.shape[0]
    index = jnp.arange(count, dtype=jnp.int32)
    shard = index // span
    offset = index % span
    key_pos = jnp.where(
        offset < pre_dev, shard * pre_dev + offset, prefix + shard * rows + offset - pre_dev
    )
    inner = 0
    g_head = first_head + inner
    visible = visible_mask(key_pos, query_pos, retrieval[g_head], sinks[g_head], windows[g_head])
    updated = [
        maybe_attend(start_state[inner], query_groups[:, inner], key_piece, value_piece, visible)
    ]
    final = tuple(updated)
    pieces = [final[0][2] / final[0][1][..., None]]
    result = jnp.stack(pieces, 1).reshape(rows, local_kv * group * DH).astype(jnp.bfloat16)
    return lax.all_to_all(result, "head", split_axis=0, concat_axis=1, tiled=True)


def solution(mesh):
    in_specs = (
        P(("seq", "head"), None),
        P(("seq", "head"), None),
        P(("seq", "head"), None),
        P("seq", "head"),
        P("seq", "head"),
        P(),
        P(),
        P(),
    )
    out_specs = P(("seq", "head"), None)
    return jax.shard_map(body, mesh=mesh, in_specs=in_specs, out_specs=out_specs, check_vma=False)
```

profile of v0, /device:TPU:17, one launch (start us, length us, event | category | flops | bytes accessed | tf_op | source)
XLA Modules:
  0.0 359.5 jit_solution(2183351999219318143)
XLA Ops:
  6.5 0.0 copy-start
  6.5 0.0 all-gather.3.cloned.1.call-start
  6.5 0.9 copy-done
  7.5 10.6 %all_to_all.70 = bf16[64,8,128]{2,0,1:T(8,128)(2,1)S(1)} all-to-all(bf16[64,8,128]{2,0,1:T(8,128)(2,1)S(1)} %copy_bitcast_fusion.2), channel_id=1, replica_groups=mesh['seq'=16,'head'=8] {'head'}, dimensions={1} | all-to-all | bytes 262144 | tf_op jit(solution)/shard_map/all_to_all | solution.py:62
  18.1 1.5 pad_maximum_fusion
  19.6 0.0 all-gather.3.cloned.1.call-update
  19.6 0.0 all-gather.5.cloned.1.call-start
  19.7 0.9 copy_bitcast_fusion.1
  20.6 7.8 %all_to_all.71 = bf16[64,8,128]{2,0,1:T(8,128)(2,1)S(1)} all-to-all(bf16[64,8,128]{2,0,1:T(8,128)(2,1)S(1)} %copy_bitcast_fusion.1), channel_id=1, replica_groups=mesh['seq'=16,'head'=8] {'head'}, dimensions={1} | all-to-all | bytes 262144 | tf_op jit(solution)/shard_map/all_to_all | solution.py:63
  28.5 1.5 pad_maximum_fusion.1
  30.0 0.0 all-gather.5.cloned.1.call-update
  30.0 2.3 copy.43
  32.3 3.6 all-to-all-start
  35.9 1.3 dynamic_slice.11
  37.2 1.3 dynamic_slice.10
  38.4 1.2 dynamic_slice.9
  40.2 0.6 iota_add_fusion
  40.9 0.7 compare_or_fusion
  41.6 10.1 %fusion.24 = (pred[]{:T(512)}, pred[512,12288]{1,0:T(8,128)(4,1)}) fusion(s32[512]{0:T(512)S(1)} %get-tuple-element.38, pred[12288]{0:T(1024)(128)(4,1)S(1)} %compare_or_fusion, s32[512]{0:T(512)S(1)} %get-tuple-element.37, s32[12288]{0:T(1024)S(1)} %fusion.21), kind=kLoop, calls=%fused_computation.40 | loop fusion | flops 31457280 | bytes 6356993 | tf_op jit(solution)/shard_map/reduce_or | solution.py:34
  52.4 0.0 all-to-all-done
  52.4 0.3 copy.35
  52.7 19.7 %all-gather.3.cloned.1.call-done = bf16[12288,128]{1,0:T(8,128)(2,1)} async-done(((bf16[768,128]{1,0:T(8,128)(2,1)}), bf16[12288,128]{1,0:T(8,128)(2,1)}) %all-gather.3.cloned.1.call-update) | async-done | bytes 3145744 | tf_op jit(solution)/shard_map/all_gather | solution.py:72
  72.4 53.4 %all-gather.5.cloned.1.call-done = bf16[12288,128]{1,0:T(8,128)(2,1)} async-done(((bf16[768,128]{1,0:T(8,128)(2,1)}), bf16[12288,128]{1,0:T(8,128)(2,1)}) %all-gather.5.cloned.1.call-update) | async-done | bytes 3145744 | tf_op jit(solution)/shard_map/all_gather | solution.py:73
  125.8 203.0 %conditional.1 = (f32[512,8]{0,1:T(8,128)}, f32[512,8,128]{2,0,1:T(8,128)}) conditional(s32[]{:T(128)} %convert_element_type.13, () %tuple.13, (pred[512,12288]{1,0:T(8,128)(4,1)}, bf16[512,8,128]{2,1,0:T(8,128)(2,1)S(1)}, bf16[12288,128]{1,0:T(8,128)(2,1)}, bf16[12288,128]{1,0:T(8,128)(2,1)}) %tuple.27), branch_computations={%region_1.2_spmd, %region_2.5_spmd} | conditional | flops 26323447808 | bytes 632389632 | solution.py:33
  125.8 69.5 %fusion = (f32[512,8]{0,1:T(8,128)S(1)}, f32[512,8,12288]{2,0,1:T(8,128)}) fusion(pred[512,12288]{1,0:T(8,128)(4,1)} %get-tuple-element.13, bf16[12288,128]{1,0:T(8,128)(2,1)} %get-tuple-element.15, bf16[512,8,128]{2,1,0:T(8,128)(2,1)S(1)} %get-tuple-element.30), kind=kOutput, calls=%fused_computation.2 | convolution fusion | flops 13035892736 | bytes 211828736 | tf_op jit(solution)/shard_map/cond/branch_1_fun/tqd,rd->tqr/dot_general | solution.py:21
  195.3 67.9 %fusion.3 = f32[512,8,128]{2,0,1:T(8,128)} fusion(f32[512,8,12288]{2,0,1:T(8,128)} %get-tuple-element.36, f32[512,8]{0,1:T(8,128)S(1)} %broadcast_maximum_fusion, pred[512,12288]{1,0:T(8,128)(4,1)} %get-tuple-element.13, bf16[12288,128]{1,0:T(8,128)(2,1)} %get-tuple-element.16), kind=kOutput, calls=%fused_computation.5 | convolution fusion | flops 13086228480 | bytes 212877312 | tf_op jit(solution)/shard_map/cond/branch_1_fun/tqr,rd->tqd/dot_general | solution.py:28
  263.2 65.6 %fusion.2 = f32[512,8]{0,1:T(8,128)} fusion(f32[512,8,12288]{2,0,1:T(8,128)} %get-tuple-element.36, f32[512,8]{0,1:T(8,128)S(1)} %broadcast_maximum_fusion, pred[512,12288]{1,0:T(8,128)(4,1)} %get-tuple-element.13), kind=kLoop, calls=%fused_computation.4 | loop fusion | flops 201322496 | bytes 207650816 | tf_op jit(solution)/shard_map/cond/branch_1_fun/reduce_sum | solution.py:26
  328.7 2.0 divide_convert_fusion
  330.7 0.7 copy.29
  331.4 0.5 convert_element_type.15
  331.9 19.7 %all_to_all.72 = bf16[8,64,1024]{2,1,0:T(8,128)(2,1)S(1)} all-to-all(bf16[8,64,1024]{2,1,0:T(8,128)(2,1)S(1)} %convert_element_type.15), channel_id=1, replica_groups=mesh['seq'=16,'head'=8] {'head'}, dimensions={0} | all-to-all | bytes 2097152 | tf_op jit(solution)/shard_map/all_to_all | solution.py:90
  351.6 1.1 copy.34
  (3 shorter events, 0.1 us)
Async XLA Ops:
  6.5 0.9 copy-start
  6.5 65.9 %all-gather.3.cloned.1.call-start = ((), (), s32[]{:S(2)}) async-start(), calls=%async_computation.4 | async-start | bytes 3342336 | tf_op jit(solution)/shard_map/all_gather | solution.py:72
  19.6 106.1 %all-gather.5.cloned.1.call-start = ((), (), s32[]{:S(2)}) async-start(), calls=%async_computation.5 | async-start | bytes 3342336 | tf_op jit(solution)/shard_map/all_gather | solution.py:73
  32.3 20.1 %all-to-all-start = ((bf16[64,8,1024]{2,0,1:T(8,128)(2,1)}), bf16[64,8,1024]{2,0,1:T(8,128)(2,1)S(1)}, u32[]{:S(2)}, u32[]{:S(2)}) async-start(bf16[64,8,1024]{2,0,1:T(8,128)(2,1)} %bitcast.37), calls=%async_computation | async-start | bytes 2097152 | tf_op jit(solution)/shard_map/all_to_all | solution.py:61
Sparse Core Ops, SparseCore 0:
  19.8 52.6 all-gather.2
  74.8 50.9 all-gather.4
where the time goes:
time: 363 us; the launch traced here: 360 us
  matrix products  137 us (38%)
  other arithmetic  82 us (23%)
  waiting for transfers between devices  73.1 us (20%)
  blocking collectives  38.2 us (11%)
  between operations  14.8 us (4%)
  local copies, waits for them, and re-layouts  10.4 us (3%)
    dot_general x1, matrix products, attend_piece(): jnp.einsum('tqd,rd->tqr', query_group, key_rows, preferred_element_type=j...  69.5 us
    dot_general x1, matrix products, attend_piece(): jnp.einsum('tqr,rd->tqd', weights, value_rows, preferred_element_type=jnp...  67.9 us
    reduce_sum x1, other arithmetic, attend_piece(): total = jnp.sum(expo, -1)  65.6 us
    all_gather x1, waiting for transfers between devices, body(): value_piece = lax.all_gather(value_block, 'seq', axis=0, tiled=True)  53.4 us
    all_to_all x1, blocking collectives, body(): lax.all_to_all(result, 'head', split_axis=0, concat_axis=1, tiled=True)  19.7 us
    all_gather x1, waiting for transfers between devices, body(): key_piece = lax.all_gather(key_block, 'seq', axis=0, tiled=True)  19.7 us
    all_to_all x1, blocking collectives, body(): lax.all_to_all(new_keys, 'head', split_axis=1, concat_axis=0, tiled=True)  10.6 us
    reduce_or x1, other arithmetic, maybe_attend(): jnp.any(visible)  10.1 us
  transfers between devices with their start and end apart: 3, of which 2 were waited for; matrix products, arithmetic and copies ran while one was open for 6% of the time, Pallas kernels for 0%

commit v1 on v0

v1 whole, which is shorter than its diff:
```python
import functools
import math

import jax
import jax.numpy as jnp
from jax import lax
from jax.experimental import pallas as pl
from jax.experimental.pallas import tpu as pltpu
from jax.sharding import PartitionSpec as P

HQ = 64
KVH = 8
DH = 128
GROUP = HQ // KVH
WIDE = GROUP * DH
SINKS = 64

SEQ, HEAD = 16, 8
TOK = 64
BLOCK = TOK * HEAD
PRE = 256
CARRY = BLOCK + SINKS
WINDOW_BLOCKS = 3

RING = 4
KEY_PARTS = 2
PIECE = TOK * RING
R_NEW_DEV = TOK // KEY_PARTS
R_NEW = BLOCK // KEY_PARTS
R_PRE = PRE // KEY_PARTS
R_SEND = R_NEW_DEV + R_PRE
R_ROWS = R_NEW + R_PRE
R_UNITS = 4
R_LANES = WIDE + DH

LOG2E_SCALED = math.log2(math.e) / math.sqrt(DH)
HIDDEN = -1e30
NT = (((1,), (1,)), ((), ()))

SMEM = pl.BlockSpec(memory_space=pltpu.SMEM)
bf16 = jnp.bfloat16
f32 = jnp.float32


VMEM = pl.BlockSpec(memory_space=pltpu.VMEM)


def call(kernel, outs, ins, flops=0, nbytes=2**20, scratch=(), vmem=44):
    def spec(a):
        if a.dtype == jnp.int32:
            return SMEM
        return VMEM if a.dtype == f32 else pl.BlockSpec(a.shape, lambda i: (0,) * len(a.shape))

    return pl.pallas_call(
        kernel,
        grid=(1,),
        out_shape=outs,
        in_specs=[spec(a) for a in ins],
        out_specs=jax.tree.map(spec, outs),
        scratch_shapes=list(scratch),
        compiler_params=pltpu.CompilerParams(vmem_limit_bytes=vmem * 2**20),
        cost_estimate=pl.CostEstimate(flops=flops, bytes_accessed=nbytes, transcendentals=0),
    )(*ins)


def retrieval_groups(flags):
    low = jnp.int32(0)
    high = jnp.int32(0)
    for g in range(KVH):
        high = jnp.where(flags[g] == 1, g, high)
        low = jnp.where(flags[KVH - 1 - g] == 1, KVH - 1 - g, low)
    return low, high


def pack_kv_kernel(flags, nk, nv, ck, cv, out, cache):
    groups = retrieval_groups(flags)
    cache[:, 0:DH] = ck[...]
    cache[:, DH:] = cv[...]
    for h in range(HEAD):
        out[h, 0:TOK, 0:DH] = nk[:, h * DH : (h + 1) * DH]
        out[h, 0:TOK, DH:] = nv[:, h * DH : (h + 1) * DH]
        x = h % RING
        cols = pl.ds(pl.multiple_of(groups[x // KEY_PARTS] * DH, DH), DH)
        part = x % KEY_PARTS
        rows = slice(part * R_NEW_DEV, (part + 1) * R_NEW_DEV)
        end = TOK + R_NEW_DEV
        out[h, TOK:end, 0:DH] = nk[rows, cols]
        out[h, TOK:end, DH:] = nv[rows, cols]
        rows = slice(part * R_PRE, (part + 1) * R_PRE)
        out[h, end:, 0:DH] = ck[rows, :]
        out[h, end:, DH:] = cv[rows, :]


def unpack_kv_kernel(flags, place, got, cache, first, second, third, part, own, two_on, odd_on):
    s = place[0]
    low, high = retrieval_groups(flags)
    source = jnp.where((place[1] % RING) // KEY_PARTS == 0, low, high)
    end = TOK + R_NEW_DEV
    part[0:R_PRE, :] = got[source, end:, :]
    part[R_PRE:, :] = got[:, TOK:end, :].reshape(R_NEW, 2 * DH)
    whole = got[:, 0:TOK, :].reshape(BLOCK, 2 * DH)
    last = s == SEQ - 1
    sink = jnp.where(
        s == 0,
        cache[0:SINKS],
        jnp.where(s == 4, second[0:SINKS], jnp.where(s == 8, first[0:SINKS], third[0:SINKS])),
    )
    for out in (own, two_on, odd_on):
        out[BLOCK:, :] = sink
    own[0:BLOCK, :] = whole
    for shift, over in ((two_on, s + 2 >= SEQ), (odd_on, (s % 2 == 1) & (s + 3 >= SEQ))):

        @pl.when(jnp.logical_not(over))
        def _():
            shift[0:BLOCK, :] = whole

        @pl.when(over)
        def _():
            shift[0:PRE, :] = first[...]
            shift[PRE:BLOCK, :] = jnp.where(last, cache[...], second[...])


def pack_q_kernel(flags, place, q, out, *rings):
    low, high = retrieval_groups(flags)
    for k, ring in enumerate(rings):
        other = (place[1] + k) % RING
        start = pl.multiple_of(jnp.where(other // KEY_PARTS == 0, low, high) * WIDE, WIDE)
        ring[...] = q[:, pl.ds(start, WIDE)]
    for h in range(HEAD):
        out[h] = q[:, h * WIDE : (h + 1) * WIDE]


P_TILE = 256
P_SPAN = WINDOW_BLOCKS * BLOCK + P_TILE
P_KEYS = P_SPAN + DH


def passing_kernel(place, flags, sinks, windows, q, far, two, near, own, out, kbuf, vbuf, kt, vt, bias):
    s, h = place[0], place[1]
    odd = s % 2

    @pl.when(flags[h] == 0)
    def _():
        n_sink, window = sinks[h], windows[h]
        for i, b in ((2 * odd, near), (1, two), (2 - 2 * odd, far), (3, own)):
            rows = pl.ds(pl.multiple_of(i * BLOCK, BLOCK), BLOCK)
            kbuf[rows, :] = b[0:BLOCK, 0:DH]
            vbuf[rows, :] = b[0:BLOCK, DH:]
        sink = own[BLOCK:, :]
        for i, b in ((1, near), (2, two), (3, far)):
            sink = jnp.where(s % 4 == i, b[BLOCK:, :], sink)
        kt[P_SPAN : P_SPAN + SINKS, :] = sink[:, 0:DH]
        kt[P_SPAN + SINKS :, :] = jnp.zeros((DH - SINKS, DH), bf16)
        vt[P_SPAN : P_SPAN + SINKS, 0:DH] = sink[:, DH:]
        vt[P_SPAN + SINKS :, 0:DH] = jnp.zeros((DH - SINKS, DH), bf16)
        vt[:, DH:] = jnp.ones((P_KEYS, DH), bf16)

        def tile(t, _):
            rows = pl.ds(pl.multiple_of(t * P_TILE, P_TILE), P_SPAN)
            kt[0:P_SPAN, :] = kbuf[rows, :]
            vt[0:P_SPAN, 0:DH] = vbuf[rows, :]
            row = lax.broadcasted_iota(jnp.int32, (P_TILE, P_KEYS), 0) + WINDOW_BLOCKS * BLOCK
            col = lax.broadcasted_iota(jnp.int32, (P_TILE, P_KEYS), 1)
            seen = jnp.where(
                col < P_SPAN,
                jnp.where((col <= row) & (col > row - window), 0.0, HIDDEN),
                jnp.where(col - P_SPAN < n_sink, 0.0, HIDDEN),
            )
            bias[...] = seen
            places = pl.ds(t * (P_TILE // TOK), P_TILE // TOK)

            def scores(i):
                qi = q[places, :, i * DH : (i + 1) * DH].reshape(P_TILE, DH)
                return lax.dot_general(qi, kt[...], NT, preferred_element_type=f32)

            s = scores(0)
            for i in range(GROUP):
                ahead = scores(i + 1) if i + 1 < GROUP else None
                s = s + bias[...]
                top = jnp.max(s, -1, keepdims=True)
                p = jnp.exp2(s * LOG2E_SCALED - top * LOG2E_SCALED).astype(bf16)
                acc = jnp.dot(p, vt[...], preferred_element_type=f32)
                o = (acc[:, 0:DH] / acc[:, DH:]).astype(bf16)
                out[places, :, i * DH : (i + 1) * DH] = o.reshape(P_TILE // TOK, TOK, DH)
                s = ahead
            return 0

        lax.fori_loop(0, BLOCK // P_TILE, tile, 0)


R_CHUNK = 1024
R_KEYS = SEQ * R_ROWS // 2
R_QUERIES = 2 * PIECE


def retrieval_kernel(own_core, place, *refs):
    rings, refs = refs[:RING], refs[RING:]
    if own_core:
        *chunks, acc, top, kbuf, vbuf, qbuf, bias = refs
    else:
        *chunks, old_acc, old_top, out, kbuf, vbuf, qbuf, acc, top = refs
    s, h = place[0], place[1]
    part = h % KEY_PARTS
    y, zc = s // 4, s % 4
    core = zc % 2 if own_core else 1 - zc % 2
    diagonal = R_NEW if own_core else 0
    fixed = diagonal + SEQ // 2 * R_PRE
    vbuf[:, DH:] = jnp.ones((R_KEYS, DH), bf16)
    for back, chunk in enumerate(chunks):
        for dz in range(2):
            zh = zc // 2 if dz == 0 else 1 - zc // 2
            pair = ((y + 4 - back) % 4) * 2 + zh
            other = 2 * pair + core
            base = dz * R_ROWS
            to = diagonal + (2 * back + dz) * R_PRE
            kbuf[to : to + R_PRE, :] = chunk[base : base + R_PRE, 0:DH]
            vbuf[to : to + R_PRE, 0:DH] = chunk[base : base + R_PRE, DH:]
            new = chunk[base + R_PRE : base + R_ROWS, :]
            if own_core and back == 0 and dz == 0:
                kbuf[0:R_NEW, :] = new[:, 0:DH]
                vbuf[0:R_NEW, 0:DH] = new[:, DH:]
            new = jnp.where(other < s, new, jnp.zeros_like(new))

            @pl.when(fixed + pair * R_NEW < R_KEYS)
            def _():
                to = pl.ds(pl.multiple_of(fixed + pair * R_NEW, R_NEW), R_NEW)
                kbuf[to, :] = new[:, 0:DH]
                vbuf[to, 0:DH] = new[:, DH:]

    for k, ring in enumerate(rings):
        x = (h + RING - k) % RING
        for i in range(GROUP):
            to = pl.ds(pl.multiple_of((i % 2) * PIECE + x * TOK, TOK), TOK)
            qbuf[i // 2, to, :] = ring[:, i * DH : (i + 1) * DH]
    count = fixed + (s // 2 + (0 if own_core else zc % 2)) * R_NEW
    steps = (count + R_CHUNK - 1) // R_CHUNK
    if own_core:
        token = lax.broadcasted_iota(jnp.int32, (R_QUERIES, R_NEW), 0) % PIECE + (h // RING) * PIECE
        col = lax.broadcasted_iota(jnp.int32, (R_QUERIES, R_NEW), 1)
        key = (col // R_NEW_DEV) * TOK + part * R_NEW_DEV + col % R_NEW_DEV
        bias[...] = jnp.where(key <= token, 0.0, HIDDEN)
    else:
        acc[...] = old_acc[...]
        top[...] = old_top[...]

    def scores(i, keys):
        return lax.dot_general(qbuf[i], keys, NT, preferred_element_type=f32)

    def step(j, kind):
        if kind == "first":
            rows = slice(0, R_CHUNK)
        else:
            rows = pl.ds(pl.multiple_of(j * R_CHUNK, R_CHUNK), R_CHUNK)
        keys = kbuf[rows, :]
        values = vbuf[rows, :]
        if kind == "last":
            at = lax.broadcasted_iota(jnp.int32, (1, R_CHUNK), 1) + j * R_CHUNK
            tail = jnp.where(at < count, 0.0, HIDDEN)
        s_now = scores(0, keys)
        for i in range(R_UNITS):
            ahead = scores(i + 1, keys) if i + 1 < R_UNITS else None
            if kind == "first":
                s_now = jnp.concatenate([s_now[:, 0:R_NEW] + bias[...], s_now[:, R_NEW:]], 1)
            if kind == "last":
                s_now = s_now + tail
            peak = jnp.max(s_now, -1, keepdims=True)
            if kind == "first":
                fresh = peak
            else:
                old = top[i][:, 0:1]
                fresh = jnp.maximum(old, peak)
                shrink = jnp.exp2((old - fresh) * LOG2E_SCALED)
            p = jnp.exp2(s_now * LOG2E_SCALED - fresh * LOG2E_SCALED).astype(bf16)
            d = jnp.dot(p, values, preferred_element_type=f32)
            if kind != "first":
                d = acc[i] * shrink + d
            top[i] = jnp.broadcast_to(fresh, (R_QUERIES, DH))
            acc[i] = d
            s_now = ahead

    def middle(j, _):
        step(j, "middle")
        return 0

    if own_core:
        step(0, "first")
    lax.fori_loop(1 if own_core else 0, steps - 1, middle, 0)
    step(steps - 1, "last")
    if own_core:
        return

    lane = lax.broadcasted_iota(jnp.int32, (PIECE, DH), 1)
    logs = jnp.zeros((PIECE, DH), f32)
    for i in range(GROUP):
        rows = slice((i % 2) * PIECE, (i % 2 + 1) * PIECE)
        total = acc[i // 2, rows, DH:]
        o = (acc[i // 2, rows, 0:DH] / total).astype(bf16)
        out[:, :, i * DH : (i + 1) * DH] = o.reshape(RING, TOK, DH)
        log = top[i // 2, rows] * LOG2E_SCALED + jnp.log2(total)
        hi = log.astype(bf16).astype(f32)
        mid = (log - hi).astype(bf16).astype(f32)
        lo = log - hi - mid
        logs = jnp.where(lane == 3 * i, hi, logs)
        logs = jnp.where(lane == 3 * i + 1, mid, logs)
        logs = jnp.where(lane == 3 * i + 2, lo, logs)
    out[:, :, WIDE:] = logs.astype(bf16).reshape(RING, TOK, DH)


def finish_kernel(flags, passing, partial, out):
    groups = retrieval_groups(flags)
    for g in range(KVH):

        @pl.when(flags[g] == 0)
        def _():
            out[:, g * WIDE : (g + 1) * WIDE] = passing[g]

    for which in range(2):
        pieces = [partial[which * KEY_PARTS + kp] for kp in range(KEY_PARTS)]
        for i in range(GROUP):
            logs = []
            for piece in pieces:
                l3 = piece[:, WIDE + 3 * i : WIDE + 3 * i + 3].astype(f32)
                logs.append(l3[:, 0:1] + l3[:, 1:2] + l3[:, 2:3])
            top = functools.reduce(jnp.maximum, logs)
            shares = [jnp.exp2(x - top) for x in logs]
            total = functools.reduce(jnp.add, shares)
            o = sum(
                piece[:, i * DH : (i + 1) * DH].astype(f32) * (share / total)
                for piece, share in zip(pieces, shares)
            )
            start = groups[which] * WIDE + i * DH
            out[:, pl.ds(pl.multiple_of(start, DH), DH)] = o.astype(bf16)


def swap(x, axis):
    return lax.all_to_all(x, axis, split_axis=0, concat_axis=0, tiled=True)


def body(queries, new_keys, new_values, cache_keys, cache_values, retrieval, sinks, windows):
    column_index = lax.axis_index("zl") * RING + lax.axis_index("x")
    place = jnp.stack([lax.axis_index("seq"), column_index]).astype(jnp.int32)

    def send(x, pairs):
        return lax.ppermute(x, "seq", pairs)

    sds = jax.ShapeDtypeStruct
    two = 2 * DH
    packed, cache = call(
        pack_kv_kernel,
        (sds((HEAD, TOK + R_SEND, two), bf16), sds((PRE, two), bf16)),
        (retrieval, new_keys, new_values, cache_keys, cache_values),
        vmem=60,
    )
    got = swap(packed, ("zl", "x"))
    first = send(cache, [(10, 13), (12, 14), (14, 15), (0, 8)])
    second = send(cache, [(11, 13), (13, 14), (0, 4)])
    third = send(cache, [(0, 12)])
    ring = sds((TOK, WIDE), bf16)
    packed_q, *rings = call(
        pack_q_kernel,
        (sds((HEAD, TOK, WIDE), bf16), ring, ring, ring, ring),
        (retrieval, place, queries),
        nbytes=2**22,
        vmem=60,
    )
    rings = rings[:1] + [
        lax.ppermute(rings[k], "x", [(i, (i + k) % RING) for i in range(RING)]) for k in (1, 2, 3)
    ]
    got, first, second, third, packed_q, *rings = lax.optimization_barrier(
        (got, first, second, third, packed_q, *rings)
    )
    rows = sds((CARRY, two), bf16)
    part, own, two_on, odd_on = call(
        unpack_kv_kernel,
        (sds((R_ROWS, two), bf16), rows, rows, rows),
        (retrieval, place, got, cache, first, second, third),
    )
    cells = [(y, zh, c) for y in range(4) for zh in range(2) for c in range(2)]
    back_z = send(part, [(4 * y + 2 * z + c, 4 * y + 2 * (1 - z) + c) for y, z, c in cells])
    column = jnp.concatenate([part, back_z], 0)
    own_core = [column] + [send(column, [(i, (i + 4 * k) % SEQ) for i in range(SEQ)]) for k in (1, 2, 3)]
    two_on, odd_on, packed_q, own_core[1] = lax.optimization_barrier(
        (two_on, odd_on, packed_q, own_core[1])
    )
    q = swap(packed_q, ("zl", "x"))
    back_two = send(two_on, [(i, (i + 2) % SEQ) for i in range(SEQ)])
    near = send(odd_on, [(i, i + 1 if i % 2 == 0 else (i + 3) % SEQ) for i in range(SEQ)])
    other_core = [send(x, [(i, i ^ 1) for i in range(SEQ)]) for x in own_core]

    state = [
        sds((R_UNITS, R_QUERIES, 2 * DH), f32),
        sds((R_UNITS, R_QUERIES, DH), f32),
    ]
    buffers = [
        pltpu.VMEM((R_KEYS, DH), bf16),
        pltpu.VMEM((R_KEYS, 2 * DH), bf16),
        pltpu.VMEM((R_UNITS, R_QUERIES, DH), bf16),
    ]
    flops = R_UNITS * R_QUERIES * R_KEYS * 4 * DH
    acc, top = call(
        functools.partial(retrieval_kernel, True),
        state,
        (place, *rings, *own_core),
        flops=flops,
        nbytes=2**22,
        scratch=buffers + [pltpu.VMEM((R_QUERIES, R_NEW), f32)],
    )
    acc, top, back_two, *other_core = lax.optimization_barrier((acc, top, back_two, *other_core))
    far = send(back_two, [(i, i ^ 1) for i in range(SEQ)])
    partial = call(
        functools.partial(retrieval_kernel, False),
        sds((RING, TOK, R_LANES), bf16),
        (place, *rings, *other_core, acc, top),
        flops=flops,
        nbytes=2**22,
        scratch=buffers + [pltpu.VMEM(a.shape, f32) for a in state],
    )
    partial, q, far, near = lax.optimization_barrier((partial, q, far, near))
    partial_back = swap(partial, "x")
    pairs = BLOCK * GROUP * P_KEYS
    passing = call(
        passing_kernel,
        sds((HEAD, TOK, WIDE), bf16),
        (place, retrieval, sinks, windows, q, far, back_two, near, own),
        flops=pairs * 4 * DH,
        nbytes=2**22,
        scratch=[
            pltpu.VMEM((4 * BLOCK, DH), bf16),
            pltpu.VMEM((4 * BLOCK, DH), bf16),
            pltpu.VMEM((P_KEYS, DH), bf16),
            pltpu.VMEM((P_KEYS, 2 * DH), bf16),
            pltpu.VMEM((P_TILE, P_KEYS), f32),
        ],
    )
    passing, partial_back = lax.optimization_barrier((passing, partial_back))
    passing_back = swap(passing, ("zl", "x"))
    step = TOK // 4
    return pl.pallas_call(
        finish_kernel,
        grid=(TOK // step,),
        out_shape=sds((TOK, HQ * DH), bf16),
        in_specs=[
            SMEM,
            pl.BlockSpec((HEAD, step, WIDE), lambda i: (0, i, 0)),
            pl.BlockSpec((RING, step, R_LANES), lambda i: (0, i, 0)),
        ],
        out_specs=pl.BlockSpec((step, HQ * DH), lambda i: (i, 0)),
        compiler_params=pltpu.CompilerParams(vmem_limit_bytes=56 * 2**20),
        cost_estimate=pl.CostEstimate(flops=0, bytes_accessed=2**22, transcendentals=0),
    )(retrieval, passing_back, partial_back)


def solution(mesh):
    cut = jax.sharding.Mesh(mesh.devices.reshape(SEQ, 2, RING), ("seq", "zl", "x"))
    tokens = P(("seq", "zl", "x"), None)
    cache = P("seq", ("zl", "x"))
    return jax.shard_map(
        body,
        mesh=cut,
        in_specs=(tokens, tokens, tokens, cache, cache, P(), P(), P()),
        out_specs=tokens,
        check_vma=False,
    )
```

time: 363 us -> 132 us (0.36)
  matrix products: 137 us -> 0 us
  other arithmetic: 82 us -> 0.58 us
  waiting for transfers between devices: 73.1 us -> 18.9 us
  Pallas kernels: 0 us -> 46.4 us
  starting transfers between devices: 3.6 us -> 42.8 us
  blocking collectives: 38.2 us -> 18.2 us
  between operations: 14.8 us -> 0.24 us
  local copies, waits for them, and re-layouts: 10.4 us -> 4.72 us
    dot_general x2 -> x0, matrix products: 137 us -> none  [the longest x1 69.5 us: attend_piece(): jnp.einsum('tqd,rd->tqr', query_group, key_rows, preferred_element_type=j...]
    all_gather x2 -> x0, waiting for transfers between devices: 73.1 us -> none  [the longest x1 53.4 us: body(): value_piece = lax.all_gather(value_block, 'seq', axis=0, tiled=True)]
    reduce_sum x1 -> x0, other arithmetic: 65.6 us -> none  [attend_piece(): total = jnp.sum(expo, -1)]
    pallas_call x0 -> x7, Pallas kernels: none -> 46.4 us  [the longest x6 42.3 us: call(): pl.pallas_call(kernel, grid=(1,), out_shape=outs, in_specs=[spec(a) for a...]
    ppermute x0 -> x17, starting transfers between devices: none -> 26.4 us  [the longest x14 21.3 us: send(): return lax.ppermute(x, 'seq', pairs)]
    all_to_all x3 -> x1, blocking collectives: 38.2 us -> 18.2 us  [swap(): return lax.all_to_all(x, axis, split_axis=0, concat_axis=0, tiled=True)]
    ppermute x0 -> x17, waiting for transfers between devices: none -> 18.9 us  [the longest x14 10.8 us: send(): return lax.ppermute(x, 'seq', pairs)]
    all_to_all x1 -> x3, starting transfers between devices: 3.56 us -> 16.5 us  [swap(): return lax.all_to_all(x, axis, split_axis=0, concat_axis=0, tiled=True)]
  transfers between devices with their start and end apart: 3 -> 20, of which waited for: 2 -> 4; matrix products, arithmetic and copies ran while one was open for 6% -> 0% of each run, Pallas kernels for 0% -> 30%
where the time goes in v1:
time: 132 us
  Pallas kernels  46.4 us (35%)
  starting transfers between devices  42.8 us (32%)
  waiting for transfers between devices  18.9 us (14%)
  blocking collectives  18.2 us (14%)
  local copies, waits for them, and re-layouts  4.72 us (4%)
    pallas_call x6, Pallas kernels, call(): pl.pallas_call(kernel, grid=(1,), out_shape=outs, in_specs=[spec(a) for a...  42.3 us
    ppermute x14, starting transfers between devices, send(): return lax.ppermute(x, 'seq', pairs)  21.3 us
    all_to_all x1, blocking collectives, swap(): return lax.all_to_all(x, axis, split_axis=0, concat_axis=0, tiled=True)  18.2 us
    all_to_all x3, starting transfers between devices, swap(): return lax.all_to_all(x, axis, split_axis=0, concat_axis=0, tiled=True)  16.5 us
    ppermute x14, waiting for transfers between devices, send(): return lax.ppermute(x, 'seq', pairs)  10.8 us
    ppermute x3, waiting for transfers between devices, body(): lax.ppermute(rings[k], 'x', [(i, (i + k) % RING) for i in range(RING)])  8.13 us
    ppermute x3, starting transfers between devices, body(): lax.ppermute(rings[k], 'x', [(i, (i + k) % RING) for i in range(RING)])  5.04 us
    unnamed x41, local copies, waits for them, and re-layouts  4.71 us
  transfers between devices with their start and end apart: 20, of which 4 were waited for; matrix products, arithmetic and copies ran while one was open for 0% of the time, Pallas kernels for 30%

profile of v1, /device:TPU:17, one launch (start us, length us, event | category | flops | bytes accessed | tf_op | source)
XLA Modules:
  0.0 131.8 jit_solution(16362153961366398522)
XLA Ops:
  0.0 2.1 %shard_map.82 = (bf16[8,224,256]{2,1,0:T(8,128)(2,1)}, bf16[256,256]{1,0:T(8,128)(2,1)}) custom-call(s32[8]{0:T(128)} %flags.9, bf16[64,1024]{1,0:T(8,128)(2,1)} %nk.1, bf16[64,1024]{1,0:T(8,128)(2,1)} %nv.1, bf16[256,128]{1,0:T(8,128)(2,1)} %ck.1, bf16[256,128]{1,0:T(8,128)(2,1)} %cv.1), custom_call_target="tpu_custom_call" | custom-call | bytes 1048576 | tf_op jit(solution)/shard_map/pallas_call | solution.py:54
  2.1 5.5 %all-to-all-start = ((bf16[8,224,256]{2,1,0:T(8,128)(2,1)}), bf16[8,224,256]{2,1,0:T(8,128)(2,1)S(1)}, u32[]{:S(2)}, u32[]{:S(2)}) async-start(bf16[8,224,256]{2,1,0:T(8,128)(2,1)} %get-tuple-element.44), calls=%async_computation | async-start | bytes 1835008 | tf_op jit(solution)/shard_map/all_to_all | solution.py:336
  8.2 2.4 %shard_map.83 = (bf16[8,64,1024]{2,1,0:T(8,128)(2,1)}, bf16[64,1024]{1,0:T(8,128)(2,1)}, bf16[64,1024]{1,0:T(8,128)(2,1)}, bf16[64,1024]{1,0:T(8,128)(2,1)}, bf16[64,1024]{1,0:T(8,128)(2,1)}) custom-call(s32[8]{0:T(128)} %flags.9, s32[2]{0:T(128)} %pad_add_fusion.place, bf16[64,8192]{1,0:T(8,128)(2,1)} %q.1), custom_call_target="tpu_custom_call" | custom-call | bytes 4194304 | tf_op jit(solution)/shard_map/pallas_call | solution.py:54
  10.7 1.5 %collective-permute-start.3 = (bf16[64,1024]{1,0:T(8,128)(2,1)}, bf16[64,1024]{1,0:T(8,128)(2,1)S(1)}, u32[]{:S(2)}, u32[]{:S(2)}) collective-permute-start(bf16[64,1024]{1,0:T(8,128)(2,1)} %get-tuple-element.48), channel_id=1, source_target_pairs={{0,1},{1,2},{2,3},{3,0},{4,5},{5,6},{6,7},{7,4},{8,9},{9,10},{10,1... | collective-permute-start | bytes 393224 | tf_op jit(solution)/shard_map/ppermute | solution.py:367
  12.1 2.4 %collective-permute-start.4 = (bf16[64,1024]{1,0:T(8,128)(2,1)}, bf16[64,1024]{1,0:T(8,128)(2,1)S(1)}, u32[]{:S(2)}, u32[]{:S(2)}) collective-permute-start(bf16[64,1024]{1,0:T(8,128)(2,1)} %get-tuple-element.49), channel_id=1, source_target_pairs={{0,2},{1,3},{2,0},{3,1},{4,6},{5,7},{6,4},{7,5},{8,10},{9,11},{10,... | collective-permute-start | bytes 393224 | tf_op jit(solution)/shard_map/ppermute | solution.py:367
  14.5 1.2 collective-permute-start.5
  15.7 0.7 collective-permute-start
  16.4 0.7 collective-permute-start.1
  17.0 7.5 %collective-permute-done.3.refs_1_ = bf16[64,1024]{1,0:T(8,128)(2,1)S(1)} collective-permute-done((bf16[64,1024]{1,0:T(8,128)(2,1)}, bf16[64,1024]{1,0:T(8,128)(2,1)S(1)}, u32[]{:S(2)}, u32[]{:S(2)}) %collective-permute-start.3) | collective-permute-done | bytes 131104 | tf_op jit(solution)/shard_map/ppermute | solution.py:367
  24.6 0.7 collective-permute-start.2
  25.8 0.7 copy-done.12
  26.5 0.7 copy-done.15
  27.2 0.6 copy-done.2
  27.8 0.6 shard_map.84
  28.5 3.4 %collective-permute-start.6 = (bf16[384,256]{1,0:T(8,128)(2,1)S(1)}, bf16[384,256]{1,0:T(8,128)(2,1)S(1)}, u32[]{:S(2)}, u32[]{:S(2)}) collective-permute-start(bf16[384,256]{1,0:T(8,128)(2,1)S(1)} %get-tuple-element.59), channel_id=1, source_target_pairs={{0,16},{8,24},{16,0},{24,8},{32,48},{40,56},{48,32},{56,40},{64,80... | collective-permute-start | bytes 589832 | tf_op jit(solution)/shard_map/ppermute | solution.py:344
  31.9 3.0 %collective-permute-done.6 = bf16[384,256]{1,0:T(8,128)(2,1)S(1)} collective-permute-done((bf16[384,256]{1,0:T(8,128)(2,1)S(1)}, bf16[384,256]{1,0:T(8,128)(2,1)S(1)}, u32[]{:S(2)}, u32[]{:S(2)}) %collective-permute-start.6) | collective-permute-done | bytes 196640 | tf_op jit(solution)/shard_map/ppermute | solution.py:344
  34.9 1.1 collective-permute-start.7
  36.4 0.9 collective-permute-start.9
  37.3 7.7 %collective-permute-done.7.refs_5_ = bf16[768,256]{1,0:T(8,128)(2,1)S(1)} collective-permute-done((bf16[768,256]{1,0:T(8,128)(2,1)S(1)}, bf16[768,256]{1,0:T(8,128)(2,1)S(1)}, u32[]{:S(2)}, u32[]{:S(2)}) %collective-permute-start.7) | collective-permute-done | bytes 393248 | tf_op jit(solution)/shard_map/ppermute | solution.py:344
  45.0 6.5 %all-to-all-start.1 = ((bf16[8,64,1024]{2,1,0:T(8,128)(2,1)}), bf16[8,64,1024]{2,1,0:T(8,128)(2,1)S(1)}, u32[]{:S(2)}, u32[]{:S(2)}) async-start(bf16[8,64,1024]{2,1,0:T(8,128)(2,1)} %get-tuple-element.73), calls=%async_computation.1 | async-start | bytes 2097152 | tf_op jit(solution)/shard_map/all_to_all | solution.py:336
  51.5 8.9 %collective-permute-start.11 = (bf16[768,256]{1,0:T(8,128)(2,1)S(1)}, bf16[768,256]{1,0:T(8,128)(2,1)S(1)}, u32[]{:S(2)}, u32[]{:S(2)}) collective-permute-start(bf16[768,256]{1,0:T(8,128)(2,1)S(1)} %constant_dynamic-update-slice_fusion.refs_4_), channel_id=1, source_target_pairs={{0,8},{8,0},{16,24},{24,16},{32,40},{40,32},{48,56},{56,48},{64,72... | collective-permute-start | bytes 1179656 | tf_op jit(solution)/shard_map/ppermute | solution.py:344
  61.0 3.3 %collective-permute-start.10 = (bf16[576,256]{1,0:T(8,128)(2,1)S(1)}, bf16[576,256]{1,0:T(8,128)(2,1)S(1)}, u32[]{:S(2)}, u32[]{:S(2)}) collective-permute-start(bf16[576,256]{1,0:T(8,128)(2,1)S(1)} %get-tuple-element.66), channel_id=1, source_target_pairs={{0,16},{8,24},{16,32},{24,40},{32,48},{40,56},{48,64},{56,72},{64,... | collective-permute-start | bytes 884744 | tf_op jit(solution)/shard_map/ppermute | solution.py:344
  64.3 0.9 copy-done.13
  65.2 0.9 copy-done.16
  66.2 11.8 %shard_map.85 = (f32[4,512,256]{2,1,0:T(8,128)S(1)}, f32[4,512,128]{2,1,0:T(8,128)S(1)}) custom-call(s32[2]{0:T(128)S(1)} %copy-done.2, bf16[64,1024]{1,0:T(8,128)(2,1)S(1)} %copy-done.8, bf16[64,1024]{1,0:T(8,128)(2,1)S(1)} %collective-permute-done.3.refs_1_, bf16[64,1024]{1,0:T(8,128)(2,1)S(1)} %copy-done.13, bf16[64,1024]{1,0:T(8,128)(2,1)S(1)} %copy-done.16, ...), custom_call_target="tpu_custom_call" | custom-call | flops 3221225472 | bytes 4194304 | tf_op jit(solution)/shard_map/pallas_call | solution.py:54
  78.1 0.8 collective-permute-start.15
  78.9 0.9 copy-done.11
  79.8 13.1 %shard_map.86 = bf16[4,64,1152]{2,1,0:T(8,128)(2,1)} custom-call(s32[2]{0:T(128)S(1)} %copy-done.2, bf16[64,1024]{1,0:T(8,128)(2,1)S(1)} %copy-done.9, bf16[64,1024]{1,0:T(8,128)(2,1)S(1)} %copy-done.11, bf16[64,1024]{1,0:T(8,128)(2,1)S(1)} %copy-done.14, bf16[64,1024]{1,0:T(8,128)(2,1)S(1)} %copy-done.17, ...), custom_call_target="tpu_custom_call" | custom-call | flops 3221225472 | bytes 4194304 | tf_op jit(solution)/shard_map/pallas_call | solution.py:54
  92.9 4.4 %all-to-all-start.2 = ((bf16[4,64,1152]{2,1,0:T(8,128)(2,1)}), bf16[4,64,1152]{2,1,0:T(8,128)(2,1)}, u32[]{:S(2)}, u32[]{:S(2)}) async-start(bf16[4,64,1152]{2,1,0:T(8,128)(2,1)} %shard_map.86), calls=%async_computation.2 | async-start | bytes 1179648 | tf_op jit(solution)/shard_map/all_to_all | solution.py:336
  97.4 12.2 %shard_map.87 = bf16[8,64,1024]{2,1,0:T(8,128)(2,1)S(1)} custom-call(s32[2]{0:T(128)S(1)} %copy-done.3, s32[8]{0:T(128)S(1)} %copy-done.1, s32[8]{0:T(128)S(1)} %copy-done.18, s32[8]{0:T(128)S(1)} %copy-done.19, bf16[8,64,1024]{2,1,0:T(8,128)(2,1)S(1)} %all-to-all-done.1.q, bf16[576,256]{1,0:T(8,128)(2,1)S(1)} %collective-permute-done.15.far, ...), custom_call_target="tpu_custom_call" | custom-call | flops 4026531840 | bytes 4194304 | tf_op jit(solution)/shard_map/pallas_call | solution.py:54
  109.6 18.2 %all_to_all.20.passing = bf16[8,64,1024]{2,1,0:T(8,128)(2,1)} all-to-all(bf16[8,64,1024]{2,1,0:T(8,128)(2,1)S(1)} %shard_map.87), channel_id=1, replica_groups=mesh['seq'=16,'zl'=2,'x'=4] {'zl','x'}, dimensions={0} | all-to-all | bytes 2097152 | tf_op jit(solution)/shard_map/all_to_all | solution.py:336
  127.8 4.1 %shard_map.88 = bf16[64,8192]{1,0:T(8,128)(2,1)} custom-call(s32[8]{0:T(128)} %flags.9, bf16[8,64,1024]{2,1,0:T(8,128)(2,1)} %all_to_all.20.passing, bf16[4,64,1152]{2,1,0:T(8,128)(2,1)} %all-to-all-done.2.partial), custom_call_target="tpu_custom_call" | custom-call | bytes 4194304 | tf_op jit(solution)/shard_map/pallas_call | solution.py:438
  (59 shorter events, 2.2 us)
Async XLA Ops:
  0.0 27.2 %copy-start.1 = (s32[8]{0:T(128)S(1)}, s32[8]{0:T(128)}, u32[]{:S(2)}) copy-start(s32[8]{0:T(128)} %flags.9) | copy-start | bytes 100
  2.1 13.6 %copy-start = (bf16[256,256]{1,0:T(8,128)(2,1)S(1)}, bf16[256,256]{1,0:T(8,128)(2,1)}, u32[]{:S(2)}) copy-start(bf16[256,256]{1,0:T(8,128)(2,1)} %get-tuple-element.45.cache) | copy-start | bytes 393220
  2.1 25.1 %all-to-all-start = ((bf16[8,224,256]{2,1,0:T(8,128)(2,1)}), bf16[8,224,256]{2,1,0:T(8,128)(2,1)S(1)}, u32[]{:S(2)}, u32[]{:S(2)}) async-start(bf16[8,224,256]{2,1,0:T(8,128)(2,1)} %get-tuple-element.44), calls=%async_computation | async-start | bytes 1835008 | tf_op jit(solution)/shard_map/all_to_all | solution.py:336
  10.7 13.9 %collective-permute-start.3 = (bf16[64,1024]{1,0:T(8,128)(2,1)}, bf16[64,1024]{1,0:T(8,128)(2,1)S(1)}, u32[]{:S(2)}, u32[]{:S(2)}) collective-permute-start(bf16[64,1024]{1,0:T(8,128)(2,1)} %get-tuple-element.48), channel_id=1, source_target_pairs={{0,1},{1,2},{2,3},{3,0},{4,5},{5,6},{6,7},{7,4},{8,9},{9,10},{10,1... | collective-permute-start | bytes 393224 | tf_op jit(solution)/shard_map/ppermute | solution.py:367
  12.1 13.7 %collective-permute-start.4 = (bf16[64,1024]{1,0:T(8,128)(2,1)}, bf16[64,1024]{1,0:T(8,128)(2,1)S(1)}, u32[]{:S(2)}, u32[]{:S(2)}) collective-permute-start(bf16[64,1024]{1,0:T(8,128)(2,1)} %get-tuple-element.49), channel_id=1, source_target_pairs={{0,2},{1,3},{2,0},{3,1},{4,6},{5,7},{6,4},{7,5},{8,10},{9,11},{10,... | collective-permute-start | bytes 393224 | tf_op jit(solution)/shard_map/ppermute | solution.py:367
  14.5 12.0 %collective-permute-start.5 = (bf16[64,1024]{1,0:T(8,128)(2,1)}, bf16[64,1024]{1,0:T(8,128)(2,1)S(1)}, u32[]{:S(2)}, u32[]{:S(2)}) collective-permute-start(bf16[64,1024]{1,0:T(8,128)(2,1)} %get-tuple-element.50), channel_id=1, source_target_pairs={{0,3},{1,0},{2,1},{3,2},{4,7},{5,4},{6,5},{7,6},{8,11},{9,8},{10,9... | collective-permute-start | bytes 393224 | tf_op jit(solution)/shard_map/ppermute | solution.py:367
  15.7 11.5 %collective-permute-start = (bf16[256,256]{1,0:T(8,128)(2,1)S(1)}, bf16[256,256]{1,0:T(8,128)(2,1)S(1)}, u32[]{:S(2)}, u32[]{:S(2)}) collective-permute-start(bf16[256,256]{1,0:T(8,128)(2,1)S(1)} %copy-done), channel_id=1, source_target_pairs={{80,104},{96,112},{112,120},{0,64},{81,105},{97,113},{113,121},{1,... | collective-permute-start | bytes 393224 | tf_op jit(solution)/shard_map/ppermute | solution.py:344
  16.4 10.8 %collective-permute-start.1 = (bf16[256,256]{1,0:T(8,128)(2,1)S(1)}, bf16[256,256]{1,0:T(8,128)(2,1)S(1)}, u32[]{:S(2)}, u32[]{:S(2)}) collective-permute-start(bf16[256,256]{1,0:T(8,128)(2,1)S(1)} %copy-done), channel_id=1, source_target_pairs={{88,104},{104,112},{0,32},{89,105},{105,113},{1,33},{90,106},{106,... | collective-permute-start | bytes 393224 | tf_op jit(solution)/shard_map/ppermute | solution.py:344
  24.6 39.8 %copy-start.10 = (bf16[64,1024]{1,0:T(8,128)(2,1)}, bf16[64,1024]{1,0:T(8,128)(2,1)S(1)}, u32[]{:S(2)}) copy-start(bf16[64,1024]{1,0:T(8,128)(2,1)S(1)} %collective-permute-done.3.refs_1_) | copy-start | bytes 393220
  24.6 2.6 %collective-permute-start.2 = (bf16[256,256]{1,0:T(8,128)(2,1)S(1)}, bf16[256,256]{1,0:T(8,128)(2,1)S(1)}, u32[]{:S(2)}, u32[]{:S(2)}) collective-permute-start(bf16[256,256]{1,0:T(8,128)(2,1)S(1)} %copy-done), channel_id=1, source_target_pairs={{0,96},{1,97},{2,98},{3,99},{4,100},{5,101},{6,102},{7,103}} | collective-permute-start | bytes 393224 | tf_op jit(solution)/shard_map/ppermute | solution.py:344
  27.8 36.5 %copy-start.8 = (bf16[64,1024]{1,0:T(8,128)(2,1)S(1)}, bf16[64,1024]{1,0:T(8,128)(2,1)}, u32[]{:S(2)}) copy-start(bf16[64,1024]{1,0:T(8,128)(2,1)} %get-tuple-element.51.refs_0_) | copy-start | bytes 393220
  28.4 16.5 %copy-start.4 = (bf16[576,256]{1,0:T(8,128)(2,1)}, bf16[576,256]{1,0:T(8,128)(2,1)S(1)}, u32[]{:S(2)}) copy-start(bf16[576,256]{1,0:T(8,128)(2,1)S(1)} %get-tuple-element.79.own) | copy-start | bytes 884740
  28.5 16.5 %copy-start.6 = (bf16[576,256]{1,0:T(8,128)(2,1)}, bf16[576,256]{1,0:T(8,128)(2,1)S(1)}, u32[]{:S(2)}) copy-start(bf16[576,256]{1,0:T(8,128)(2,1)S(1)} %get-tuple-element.75) | copy-start | bytes 884740
  28.5 6.4 %collective-permute-start.6 = (bf16[384,256]{1,0:T(8,128)(2,1)S(1)}, bf16[384,256]{1,0:T(8,128)(2,1)S(1)}, u32[]{:S(2)}, u32[]{:S(2)}) collective-permute-start(bf16[384,256]{1,0:T(8,128)(2,1)S(1)} %get-tuple-element.59), channel_id=1, source_target_pairs={{0,16},{8,24},{16,0},{24,8},{32,48},{40,56},{48,32},{56,40},{64,80... | collective-permute-start | bytes 589832 | tf_op jit(solution)/shard_map/ppermute | solution.py:344
  34.9 10.1 %collective-permute-start.7 = (bf16[768,256]{1,0:T(8,128)(2,1)S(1)}, bf16[768,256]{1,0:T(8,128)(2,1)S(1)}, u32[]{:S(2)}, u32[]{:S(2)}) collective-permute-start(bf16[768,256]{1,0:T(8,128)(2,1)S(1)} %constant_dynamic-update-slice_fusion.refs_4_), channel_id=1, source_target_pairs={{0,32},{8,40},{16,48},{24,56},{32,64},{40,72},{48,80},{56,88},{64,... | collective-permute-start | bytes 1179656 | tf_op jit(solution)/shard_map/ppermute | solution.py:344
  36.0 24.5 %collective-permute-start.8 = (bf16[768,256]{1,0:T(8,128)(2,1)S(1)}, bf16[768,256]{1,0:T(8,128)(2,1)S(1)}, u32[]{:S(2)}, u32[]{:S(2)}) collective-permute-start(bf16[768,256]{1,0:T(8,128)(2,1)S(1)} %constant_dynamic-update-slice_fusion.refs_4_), channel_id=1, source_target_pairs={{0,64},{8,72},{16,80},{24,88},{32,96},{40,104},{48,112},{56,120},{... | collective-permute-start | bytes 1179656 | tf_op jit(solution)/shard_map/ppermute | solution.py:344
  36.4 24.6 %collective-permute-start.9 = (bf16[768,256]{1,0:T(8,128)(2,1)S(1)}, bf16[768,256]{1,0:T(8,128)(2,1)S(1)}, u32[]{:S(2)}, u32[]{:S(2)}) collective-permute-start(bf16[768,256]{1,0:T(8,128)(2,1)S(1)} %constant_dynamic-update-slice_fusion.refs_4_), channel_id=1, source_target_pairs={{0,96},{8,104},{16,112},{24,120},{32,0},{40,8},{48,16},{56,24},{64... | collective-permute-start | bytes 1179656 | tf_op jit(solution)/shard_map/ppermute | solution.py:344
  45.0 47.9 %all-to-all-start.1 = ((bf16[8,64,1024]{2,1,0:T(8,128)(2,1)}), bf16[8,64,1024]{2,1,0:T(8,128)(2,1)S(1)}, u32[]{:S(2)}, u32[]{:S(2)}) async-start(bf16[8,64,1024]{2,1,0:T(8,128)(2,1)} %get-tuple-element.73), calls=%async_computation.1 | async-start | bytes 2097152 | tf_op jit(solution)/shard_map/all_to_all | solution.py:336
  51.5 26.5 %copy-start.7 = (bf16[576,256]{1,0:T(8,128)(2,1)S(1)}, bf16[576,256]{1,0:T(8,128)(2,1)}, u32[]{:S(2)}) copy-start(bf16[576,256]{1,0:T(8,128)(2,1)} %copy-done.6) | copy-start | bytes 884740
  51.5 27.3 %copy-start.9 = (bf16[64,1024]{1,0:T(8,128)(2,1)S(1)}, bf16[64,1024]{1,0:T(8,128)(2,1)}, u32[]{:S(2)}) copy-start(bf16[64,1024]{1,0:T(8,128)(2,1)} %get-tuple-element.51.refs_0_) | copy-start | bytes 393220
  51.5 26.4 %collective-permute-start.11 = (bf16[768,256]{1,0:T(8,128)(2,1)S(1)}, bf16[768,256]{1,0:T(8,128)(2,1)S(1)}, u32[]{:S(2)}, u32[]{:S(2)}) collective-permute-start(bf16[768,256]{1,0:T(8,128)(2,1)S(1)} %constant_dynamic-update-slice_fusion.refs_4_), channel_id=1, source_target_pairs={{0,8},{8,0},{16,24},{24,16},{32,40},{40,32},{48,56},{56,48},{64,72... | collective-permute-start | bytes 1179656 | tf_op jit(solution)/shard_map/ppermute | solution.py:344
  60.4 17.6 %collective-permute-start.12 = (bf16[768,256]{1,0:T(8,128)(2,1)S(1)}, bf16[768,256]{1,0:T(8,128)(2,1)S(1)}, u32[]{:S(2)}, u32[]{:S(2)}) collective-permute-start(bf16[768,256]{1,0:T(8,128)(2,1)S(1)} %collective-permute-done.7.refs_5_), channel_id=1, source_target_pairs={{0,8},{8,0},{16,24},{24,16},{32,40},{40,32},{48,56},{56,48},{64,72... | collective-permute-start | bytes 1179656 | tf_op jit(solution)/shard_map/ppermute | solution.py:344
  60.5 17.5 %collective-permute-start.13 = (bf16[768,256]{1,0:T(8,128)(2,1)S(1)}, bf16[768,256]{1,0:T(8,128)(2,1)S(1)}, u32[]{:S(2)}, u32[]{:S(2)}) collective-permute-start(bf16[768,256]{1,0:T(8,128)(2,1)S(1)} %collective-permute-done.8.refs_6_), channel_id=1, source_target_pairs={{0,8},{8,0},{16,24},{24,16},{32,40},{40,32},{48,56},{56,48},{64,72... | collective-permute-start | bytes 1179656 | tf_op jit(solution)/shard_map/ppermute | solution.py:344
  60.9 17.1 %collective-permute-start.14 = (bf16[768,256]{1,0:T(8,128)(2,1)S(1)}, bf16[768,256]{1,0:T(8,128)(2,1)S(1)}, u32[]{:S(2)}, u32[]{:S(2)}) collective-permute-start(bf16[768,256]{1,0:T(8,128)(2,1)S(1)} %collective-permute-done.9.refs_7_), channel_id=1, source_target_pairs={{0,8},{8,0},{16,24},{24,16},{32,40},{40,32},{48,56},{56,48},{64,72... | collective-permute-start | bytes 1179656 | tf_op jit(solution)/shard_map/ppermute | solution.py:344
  61.0 17.0 %collective-permute-start.10 = (bf16[576,256]{1,0:T(8,128)(2,1)S(1)}, bf16[576,256]{1,0:T(8,128)(2,1)S(1)}, u32[]{:S(2)}, u32[]{:S(2)}) collective-permute-start(bf16[576,256]{1,0:T(8,128)(2,1)S(1)} %get-tuple-element.66), channel_id=1, source_target_pairs={{0,16},{8,24},{16,32},{24,40},{32,48},{40,56},{48,64},{56,72},{64,... | collective-permute-start | bytes 884744 | tf_op jit(solution)/shard_map/ppermute | solution.py:344
  78.0 14.9 %collective-permute-start.16 = (bf16[576,256]{1,0:T(8,128)(2,1)S(1)}, bf16[576,256]{1,0:T(8,128)(2,1)S(1)}, u32[]{:S(2)}, u32[]{:S(2)}) collective-permute-start(bf16[576,256]{1,0:T(8,128)(2,1)S(1)} %copy-done.7), channel_id=1, source_target_pairs={{0,8},{8,32},{16,24},{24,48},{32,40},{40,64},{48,56},{56,80},{64,7... | collective-permute-start | bytes 884744 | tf_op jit(solution)/shard_map/ppermute | solution.py:344
  78.0 19.3 %copy-start.3 = (s32[2]{0:T(128)S(1)}, s32[2]{0:T(128)}, u32[]{:S(2)}) copy-start(s32[2]{0:T(128)} %pad_add_fusion.place) | copy-start | bytes 28
  78.0 19.3 %copy-start.5 = (bf16[576,256]{1,0:T(8,128)(2,1)S(1)}, bf16[576,256]{1,0:T(8,128)(2,1)}, u32[]{:S(2)}) copy-start(bf16[576,256]{1,0:T(8,128)(2,1)} %copy-done.4) | copy-start | bytes 884740
  78.1 14.8 %collective-permute-start.15 = (bf16[576,256]{1,0:T(8,128)(2,1)S(1)}, bf16[576,256]{1,0:T(8,128)(2,1)S(1)}, u32[]{:S(2)}, u32[]{:S(2)}) collective-permute-start(bf16[576,256]{1,0:T(8,128)(2,1)S(1)} %collective-permute-done.10.two), channel_id=1, source_target_pairs={{0,8},{8,0},{16,24},{24,16},{32,40},{40,32},{48,56},{56,48},{64,72... | collective-permute-start | bytes 884744 | tf_op jit(solution)/shard_map/ppermute | solution.py:344
  79.8 17.6 %copy-start.18 = (s32[8]{0:T(128)S(1)}, s32[8]{0:T(128)}, u32[]{:S(2)}) copy-start(s32[8]{0:T(128)} %sinks.1) | copy-start | bytes 100
  79.8 17.6 %copy-start.19 = (s32[8]{0:T(128)S(1)}, s32[8]{0:T(128)}, u32[]{:S(2)}) copy-start(s32[8]{0:T(128)} %windows.1) | copy-start | bytes 100
  92.9 16.7 %all-to-all-start.2 = ((bf16[4,64,1152]{2,1,0:T(8,128)(2,1)}), bf16[4,64,1152]{2,1,0:T(8,128)(2,1)}, u32[]{:S(2)}, u32[]{:S(2)}) async-start(bf16[4,64,1152]{2,1,0:T(8,128)(2,1)} %shard_map.86), calls=%async_computation.2 | async-start | bytes 1179648 | tf_op jit(solution)/shard_map/all_to_all | solution.py:336
  (8 other events, 30.0 us)
